TPU v7x, 256 devices: a whole 4x4x8 slice. The times are simulated.
256 devices in a mesh: section: 16 (over y, z_hi), tp: 16 (over z_lo, x, core).
Axes of the slice: x: 4, y: 4, z: 8 (z_hi: 4, z_lo: 2; z = z_hi * 2 + z_lo), core: 2. Of those that a mesh axis runs over, the one named last changes fastest.
Arguments:
- saved_caches: bfloat16 [16, 2, 2048, 3, 32, 128], P('section', None, 'tp'), may hold values from -100 to 100
- keeper_code: int32 [16], replicated, may hold values from 0 to 3, as said below
- result_slope: bfloat16 [16, 2048, 32, 128], P('section', 'tp'), may hold values from -6 to 6
Outputs:
- stash_grad: bfloat16 [16, 2048, 3, 32, 128], P('section', 'tp')
Inputs may be any that keep to these rules, and one draw needn't show every extreme that they name: `keeper_code`: A code below 2 names a slot of the section's own store; a code c of 2 or more names slot c - 2 of the store of section 15 - s. Every code occurs.
All inputs are finite; a program needn't handle non-finite values.
Results may differ from a plain program's by a relative error of at most 0.0073.
Values may be sent and summed in bfloat16 or wider, within the bound.
A program may use at most 128 MiB of HBM per device.

v0:
```python
import jax
import jax.numpy as jnp
from jax import lax
from jax.sharding import PartitionSpec as P


def from_partner(value, axis, stride):
    mask = 2**stride
    pairs = [(source, source ^ mask) for source in range(lax.axis_size(axis))]
    return lax.ppermute(value, axis, pairs)


def head_grads(queries, keys_in, values_in, grads_in):
    length, head_width = queries.shape
    scaling = head_width ** (-0.5)
    rows_block = 512
    blocks = length // rows_block
    col_ids = lax.broadcasted_iota(jnp.int32, (rows_block, length), 1)

    def step(totals, block_index):
        key_total, value_total = totals
        row_start = block_index * rows_block
        query_rows = lax.dynamic_slice_in_dim(queries, row_start, rows_block, 0)
        grad_rows = lax.dynamic_slice_in_dim(grads_in, row_start, rows_block, 0)
        scores = jnp.dot(query_rows, keys_in.T, preferred_element_type=jnp.float32) * scaling
        row_ids = lax.broadcasted_iota(jnp.int32, (rows_block, length), 0) + row_start
        causal = row_ids >= col_ids
        scores = jnp.where(causal, scores, jnp.float32(-1e30))
        peak = jnp.max(scores, axis=1, keepdims=True)
        expo = jnp.where(causal, jnp.exp(scores - peak), jnp.float32(0.0))
        probability = expo / jnp.sum(expo, axis=1, keepdims=True)
        weights = probability.astype(jnp.bfloat16)
        attended = jnp.dot(weights, values_in, preferred_element_type=jnp.float32)
        prob_grad = jnp.dot(grad_rows, values_in.T, preferred_element_type=jnp.float32)
        row_dots = jnp.sum(grad_rows.astype(jnp.float32) * attended, axis=1, keepdims=True)
        score_grad = (probability * (prob_grad - row_dots) * scaling).astype(jnp.bfloat16)
        query_grad = jnp.dot(score_grad, keys_in, preferred_element_type=jnp.float32)
        key_total = key_total + jnp.dot(
            score_grad.T, query_rows, preferred_element_type=jnp.float32
        )
        value_total = value_total + jnp.dot(
            weights.T, grad_rows, preferred_element_type=jnp.float32
        )
        return ((key_total, value_total), query_grad)

    zeros_init = jnp.zeros((length, head_width), jnp.float32)
    (key_grad, value_grad), query_parts = lax.scan(
        step, (zeros_init, zeros_init), jnp.arange(blocks, dtype=jnp.int32)
    )
    query_grad = query_parts.reshape(length, head_width)
    return jnp.stack([query_grad, key_grad, value_grad]).astype(jnp.bfloat16)


def attend(pieces):
    triples, grads_in = pieces
    by_head = jnp.moveaxis(triples, 2, 0)
    grad_head = jnp.moveaxis(grads_in[:, 0], 1, 0)

    def per_head(pair):
        triple, grad_one = pair
        return head_grads(triple[:, 0], triple[:, 1], triple[:, 2], grad_one)

    result = lax.map(per_head, (by_head, grad_head))
    return jnp.transpose(result, (2, 1, 0, 3))


def attend_grouped(pieces):
    triples, grads_in = pieces
    result = attend((triples[:, :, 0], grads_in[:, :, 0]))
    return result[:, :, None]


def mirror_fetch(outgoing):
    sections = lax.axis_size("section")
    fetched = outgoing
    for bit_index in range(sections.bit_length() - 1):
        fetched = from_partner(fetched, "section", bit_index)
    return fetched


def local(saved_caches, keeper_code, result_slope):
    sections = lax.axis_size("section")
    groups = lax.axis_size("tp")
    own_index = lax.axis_index("section")
    twin_segment = sections - 1 - own_index
    bucket_count = saved_caches.shape[1]
    home_flag = keeper_code[own_index]
    twin_flag = keeper_code[twin_segment]
    own_slot = lax.dynamic_index_in_dim(
        saved_caches[0], jnp.clip(home_flag, 0, bucket_count - 1), 0, keepdims=False
    )
    outgoing = lax.dynamic_index_in_dim(
        saved_caches[0], jnp.clip(twin_flag - bucket_count, 0, bucket_count - 1), 0, keepdims=False
    )
    grads_local = result_slope[0][:, None]
    token_rows, triple_count, head_count, head_width = own_slot.shape
    fetched = mirror_fetch(outgoing)
    chosen = jnp.where(home_flag >= bucket_count, fetched, own_slot)
    chosen_groups = chosen.reshape(
        token_rows, triple_count, groups, head_count // groups, head_width
    )
    grad_groups = grads_local.reshape(token_rows, 1, groups, head_count // groups, head_width)
    grouped = attend_grouped(
        (
            lax.all_to_all(chosen_groups, "tp", split_axis=2, concat_axis=0, tiled=True),
            lax.all_to_all(grad_groups, "tp", split_axis=2, concat_axis=0, tiled=True),
        )
    )
    grads = grouped.reshape(grouped.shape[0], triple_count, head_count // groups, head_width)
    returned = lax.all_to_all(grads, "tp", split_axis=0, concat_axis=2, tiled=True)
    return returned[None]


def solution(mesh):
    return jax.shard_map(
        local,
        mesh=mesh,
        in_specs=(P("section", None, "tp", None, None, None), P(), P("section", "tp", None, None)),
        out_specs=P("section", "tp", None, None, None),
        check_vma=False,
    )
```

profile of v0, /device:TPU:1, one launch (start us, length us, event | category | flops | bytes accessed | tf_op | source)
XLA Modules:
  0.0 691.2 jit_solution(4211121737437274528)
XLA Ops:
  2.6 4.1 constant_dynamic-slice_fusion.1
  7.9 3.8 collective-permute-start
  11.7 134.6 %collective-permute-done = bf16[128,3,32,128]{3,0,2,1:T(8,128)(2,1)S(1)} collective-permute-done((bf16[128,3,32,128]{3,0,2,1:T(8,128)(2,1)S(1)}, bf16[128,3,32,128]{3,0,2,1:T(8,128)(2,1)S(1)}, u32[]{:S(2)}, u32[]{:S(2)}) %collective-permute-start) | collective-permute-done | bytes 3145760 | tf_op jit(solution)/shard_map/ppermute | solution.py:10
  146.3 7.2 %collective-permute-start.1 = (bf16[128,3,32,128]{3,0,2,1:T(8,128)(2,1)S(1)}, bf16[128,3,32,128]{3,0,2,1:T(8,128)(2,1)S(1)}, u32[]{:S(2)}, u32[]{:S(2)}) collective-permute-start(bf16[128,3,32,128]{3,0,2,1:T(8,128)(2,1)S(1)} %collective-permute-done), channel_id=1, source_target_pairs={{0,32},{16,48},{32,0},{48,16},{64,96},{80,112},{96,64},{112,80},{1... | collective-permute-start | bytes 9437192 | tf_op jit(solution)/shard_map/ppermute | solution.py:10
  153.4 135.6 %collective-permute-done.1 = bf16[128,3,32,128]{3,0,2,1:T(8,128)(2,1)S(1)} collective-permute-done((bf16[128,3,32,128]{3,0,2,1:T(8,128)(2,1)S(1)}, bf16[128,3,32,128]{3,0,2,1:T(8,128)(2,1)S(1)}, u32[]{:S(2)}, u32[]{:S(2)}) %collective-permute-start.1) | collective-permute-done | bytes 3145760 | tf_op jit(solution)/shard_map/ppermute | solution.py:10
  290.5 66.7 %collective-permute-done.2 = bf16[128,3,32,128]{3,0,2,1:T(8,128)(2,1)} collective-permute-done((bf16[128,3,32,128]{3,0,2,1:T(8,128)(2,1)S(1)}, bf16[128,3,32,128]{3,0,2,1:T(8,128)(2,1)}, u32[]{:S(2)}, u32[]{:S(2)}) %collective-permute-start.2) | collective-permute-done | bytes 3145760 | tf_op jit(solution)/shard_map/ppermute | solution.py:10
  357.2 2.9 collective-permute-start.3
  360.1 2.6 copy.38
  362.7 7.1 %all-to-all-start.1 = ((bf16[128,1,16,2,128]{0,4,3,1,2:T(8,128)(2,1)}), bf16[128,1,16,2,128]{0,4,3,1,2:T(8,128)(2,1)}, u32[]{:S(2)}, u32[]{:S(2)}) async-start(bf16[128,1,16,2,128]{0,4,3,1,2:T(8,128)(2,1)} %bitcast.91), calls=%async_computation.1 | async-start | bytes 2097152 | tf_op jit(solution)/shard_map/all_to_all | solution.py:106
  370.5 55.7 %collective-permute-done.3 = bf16[128,3,32,128]{3,0,2,1:T(8,128)(2,1)} collective-permute-done((bf16[128,3,32,128]{3,0,2,1:T(8,128)(2,1)}, bf16[128,3,32,128]{3,0,2,1:T(8,128)(2,1)}, u32[]{:S(2)}, u32[]{:S(2)}) %collective-permute-start.3) | collective-permute-done | bytes 3145760 | tf_op jit(solution)/shard_map/ppermute | solution.py:10
  429.4 7.7 %all-to-all-start = ((bf16[128,3,16,2,128]{4,0,3,1,2:T(8,128)(2,1)}), bf16[128,3,16,2,128]{4,0,3,1,2:T(8,128)(2,1)}, u32[]{:S(2)}, u32[]{:S(2)}) async-start(bf16[128,3,16,2,128]{4,0,3,1,2:T(8,128)(2,1)} %copy.36), calls=%async_computation | async-start | bytes 6291456 | tf_op jit(solution)/shard_map/all_to_all | solution.py:105
  437.2 2.3 copy.39
  439.5 37.0 %all-to-all-done = bf16[128,3,16,2,128]{4,0,3,1,2:T(8,128)(2,1)} async-done(((bf16[128,3,16,2,128]{4,0,3,1,2:T(8,128)(2,1)}), bf16[128,3,16,2,128]{4,0,3,1,2:T(8,128)(2,1)}, u32[]{:S(2)}, u32[]{:S(2)}) %all-to-all-start) | async-done | bytes 3145760 | tf_op jit(solution)/shard_map/all_to_all | solution.py:105
  476.5 2.1 copy.37
  478.6 153.9 %while.26 = (s32[]{:T(128)}, bf16[2,3,2048,128]{3,2,1,0:T(8,128)(2,1)}, bf16[2,2048,3,128]{3,1,0,2:T(8,128)(2,1)S(1)}, bf16[2,2048,128]{2,1,0:T(8,128)(2,1)}, s3...) while((s32[]{:T(128)}, bf16[2,3,2048,128]{3,2,1,0:T(8,128)(2,1)}, ...), condition=%wide.region_6.7_spmd, body=%wide.region_0.6_spmd.sunk | while | flops 1640168448 | bytes 135159104 | solution.py:63
  481.8 70.6 %while.27 = (s32[]{:T(128)}, f32[2048,128]{1,0:T(8,128)}, f32[2048,128]{1,0:T(8,128)}, bf16[4,512,128]{2,1,0:T(8,128)(2,1)}, s32[4]{0:T(128)S(1)}, /*index=5*/bf...) while((s32[]{:T(128)}, f32[2048,128]{1,0:T(8,128)}, ...), condition=%wide.region_5.5_spmd.clone, body=%wide.region_1.4_spmd.clone.sunk | while | flops 1634925568 | bytes 89020872 | solution.py:47
  485.7 2.1 fusion.56
  489.8 1.9 multiply_convert_fusion.2
  491.7 2.9 convolution_add_fusion.4
  496.2 2.8 convolution_add_fusion.5
  502.8 2.1 fusion.56
  506.8 1.9 multiply_convert_fusion.2
  508.8 3.2 convolution_add_fusion.4
  513.6 3.1 convolution_add_fusion.5
  520.6 2.1 fusion.56
  524.7 1.9 multiply_convert_fusion.2
  526.7 3.2 convolution_add_fusion.4
  531.5 3.1 convolution_add_fusion.5
  538.5 2.1 fusion.56
  542.5 1.9 multiply_convert_fusion.2
  544.5 3.2 convolution_add_fusion.4
  549.3 3.1 convolution_add_fusion.5
  558.8 70.6 %while.27 = (s32[]{:T(128)}, f32[2048,128]{1,0:T(8,128)}, f32[2048,128]{1,0:T(8,128)}, bf16[4,512,128]{2,1,0:T(8,128)(2,1)}, s32[4]{0:T(128)S(1)}, /*index=5*/bf...) while((s32[]{:T(128)}, f32[2048,128]{1,0:T(8,128)}, ...), condition=%wide.region_5.5_spmd.clone, body=%wide.region_1.4_spmd.clone.sunk | while | flops 1634925568 | bytes 89020872 | solution.py:47
  562.6 2.1 fusion.56
  568.7 2.9 convolution_add_fusion.4
  573.1 2.8 convolution_add_fusion.5
  579.7 2.1 fusion.56
  585.8 3.2 convolution_add_fusion.4
  590.6 3.1 convolution_add_fusion.5
  597.6 2.1 fusion.56
  603.6 3.2 convolution_add_fusion.4
  608.4 3.1 convolution_add_fusion.5
  615.4 2.1 fusion.56
  621.5 3.2 convolution_add_fusion.4
  626.3 3.1 convolution_add_fusion.5
  632.5 6.5 copy.49
  639.1 48.3 %all_to_all.45 = bf16[2048,3,2,128]{3,2,1,0:T(2,128)(2,1)S(1)} all-to-all(bf16[2048,3,2,128]{3,2,1,0:T(2,128)(2,1)S(1)} %bitcast.88), channel_id=1, replica_groups=mesh['section'=16,'tp'=16] {'tp'}, dimensions={0} | all-to-all | bytes 6291456 | tf_op jit(solution)/shard_map/all_to_all | solution.py:110
  687.4 3.8 copy.43
  (223 shorter events, 80.4 us)
Async XLA Ops:
  7.9 138.4 %collective-permute-start = (bf16[128,3,32,128]{3,0,2,1:T(8,128)(2,1)S(1)}, bf16[128,3,32,128]{3,0,2,1:T(8,128)(2,1)S(1)}, u32[]{:S(2)}, u32[]{:S(2)}) collective-permute-start(bf16[128,3,32,128]{3,0,2,1:T(8,128)(2,1)S(1)} %bitcast.92), channel_id=1, source_target_pairs={{0,16},{16,0},{32,48},{48,32},{64,80},{80,64},{96,112},{112,96},{1... | collective-permute-start | bytes 9437192 | tf_op jit(solution)/shard_map/ppermute | solution.py:10
  146.3 142.8 %collective-permute-start.1 = (bf16[128,3,32,128]{3,0,2,1:T(8,128)(2,1)S(1)}, bf16[128,3,32,128]{3,0,2,1:T(8,128)(2,1)S(1)}, u32[]{:S(2)}, u32[]{:S(2)}) collective-permute-start(bf16[128,3,32,128]{3,0,2,1:T(8,128)(2,1)S(1)} %collective-permute-done), channel_id=1, source_target_pairs={{0,32},{16,48},{32,0},{48,16},{64,96},{80,112},{96,64},{112,80},{1... | collective-permute-start | bytes 9437192 | tf_op jit(solution)/shard_map/ppermute | solution.py:10
  289.1 68.1 %collective-permute-start.2 = (bf16[128,3,32,128]{3,0,2,1:T(8,128)(2,1)S(1)}, bf16[128,3,32,128]{3,0,2,1:T(8,128)(2,1)}, u32[]{:S(2)}, u32[]{:S(2)}) collective-permute-start(bf16[128,3,32,128]{3,0,2,1:T(8,128)(2,1)S(1)} %collective-permute-done.1), channel_id=1, source_target_pairs={{0,64},{16,80},{32,96},{48,112},{64,0},{80,16},{96,32},{112,48},{1... | collective-permute-start | bytes 9437192 | tf_op jit(solution)/shard_map/ppermute | solution.py:10
  357.2 69.0 %collective-permute-start.3 = (bf16[128,3,32,128]{3,0,2,1:T(8,128)(2,1)}, bf16[128,3,32,128]{3,0,2,1:T(8,128)(2,1)}, u32[]{:S(2)}, u32[]{:S(2)}) collective-permute-start(bf16[128,3,32,128]{3,0,2,1:T(8,128)(2,1)} %collective-permute-done.2), channel_id=1, source_target_pairs={{0,128},{16,144},{32,160},{48,176},{64,192},{80,208},{96,224},{112... | collective-permute-start | bytes 9437192 | tf_op jit(solution)/shard_map/ppermute | solution.py:10
  362.7 66.7 %all-to-all-start.1 = ((bf16[128,1,16,2,128]{0,4,3,1,2:T(8,128)(2,1)}), bf16[128,1,16,2,128]{0,4,3,1,2:T(8,128)(2,1)}, u32[]{:S(2)}, u32[]{:S(2)}) async-start(bf16[128,1,16,2,128]{0,4,3,1,2:T(8,128)(2,1)} %bitcast.91), calls=%async_computation.1 | async-start | bytes 2097152 | tf_op jit(solution)/shard_map/all_to_all | solution.py:106
  429.4 47.0 %all-to-all-start = ((bf16[128,3,16,2,128]{4,0,3,1,2:T(8,128)(2,1)}), bf16[128,3,16,2,128]{4,0,3,1,2:T(8,128)(2,1)}, u32[]{:S(2)}, u32[]{:S(2)}) async-start(bf16[128,3,16,2,128]{4,0,3,1,2:T(8,128)(2,1)} %copy.36), calls=%async_computation | async-start | bytes 6291456 | tf_op jit(solution)/shard_map/all_to_all | solution.py:105
  481.8 3.8 copy-start.4
  481.8 6.0 copy-start.2
  491.7 4.4 copy-start.1
  498.9 3.8 copy-start.4
  498.9 6.0 copy-start.2
  508.8 3.3 copy-start.8
  508.8 4.8 copy-start.1
  513.6 3.1 copy-start.3
  513.6 3.1 copy-start.5
  516.8 3.8 copy-start.4
  516.8 6.0 copy-start.2
  526.6 3.3 copy-start.8
  526.7 4.8 copy-start.1
  531.5 3.1 copy-start.3
  531.5 3.1 copy-start.5
  534.6 3.8 copy-start.4
  534.6 6.0 copy-start.2
  544.5 3.3 copy-start.8
  544.5 4.8 copy-start.1
  549.3 3.1 copy-start.3
  549.3 3.1 copy-start.5
  558.8 3.8 copy-start.4
  558.8 6.0 copy-start.2
  568.7 4.4 copy-start.1
  575.9 3.8 copy-start.4
  575.9 6.0 copy-start.2
  585.8 3.3 copy-start.8
  585.8 4.8 copy-start.1
  590.6 3.1 copy-start.3
  590.6 3.1 copy-start.5
  593.7 3.8 copy-start.4
  593.7 6.0 copy-start.2
  603.6 3.3 copy-start.8
  603.6 4.8 copy-start.1
  608.4 3.1 copy-start.3
  608.4 3.1 copy-start.5
  611.6 3.8 copy-start.4
  611.6 6.0 copy-start.2
  621.4 3.3 copy-start.8
  621.5 4.8 copy-start.1
  626.3 3.1 copy-start.3
  626.3 3.1 copy-start.5
  (30 other events, 54.6 us)
where the time goes:
time: 694 us; the launch traced here: 691 us
  waiting for transfers between devices  430 us (62%)
  matrix products  85.8 us (12%)
  local copies, waits for them, and re-layouts  53.5 us (8%)
  blocking collectives  48.3 us (7%)
  other arithmetic  35.5 us (5%)
  starting transfers between devices  30.2 us (4%)
    ppermute x4, waiting for transfers between devices, from_partner(): return lax.ppermute(value, axis, pairs)  393 us
    all_to_all x1, blocking collectives, local(): lax.all_to_all(grads, 'tp', split_axis=0, concat_axis=2, tiled=True)  48.3 us
    all_to_all x1, waiting for transfers between devices, local(): lax.all_to_all(chosen_groups, 'tp', split_axis=2, concat_axis=0, tiled=True)  37 us
    dot_general x8, matrix products, step(): jnp.dot(score_grad.T, query_rows, preferred_element_type=jnp.float32)  25.1 us
    dot_general x8, matrix products, step(): jnp.dot(weights.T, grad_rows, preferred_element_type=jnp.float32)  24.4 us
    while x144, local copies, waits for them, and re-layouts  20.5 us
    div x8, other arithmetic, step(): probability = expo / jnp.sum(expo, axis=1, keepdims=True)  17 us
    dot_general x8, matrix products, step(): jnp.dot(grad_rows, values_in.T, preferred_element_type=jnp.float32)  15.5 us
  transfers between devices with their start and end apart: 6, of which 5 were waited for; matrix products, arithmetic and copies ran while one was open for 1% of the time, Pallas kernels for 0%

commit v1 on v0

v1 whole, which is shorter than its diff:
```python
import functools

import jax
import jax.numpy as jnp
from jax import lax
from jax.experimental import pallas as pl
from jax.experimental.pallas import tpu as pltpu
from jax.sharding import PartitionSpec as P

MESH = pl.DeviceIdType.MESH
F32 = jnp.float32
BF16 = jnp.bfloat16
LOG2E = 1.4426950408889634
ROWS_BY_ROWS = (((1,), (1,)), ((), ()))
PLAIN = (((1,), (0,)), ((), ()))


def dot(a, b, dims):
    return lax.dot_general(a, b, dims, preferred_element_type=F32)


def head_backward(q, k, v, g, put, scores, slopes, key_total, value_total, k_turned, length, block):
    width = q.shape[-1]
    scaling = width ** (-0.5)
    exponent = scaling * LOG2E
    blocks = length // block
    k_turned[...] = k[...].T
    key_ids = lax.broadcasted_iota(jnp.int32, (block, block), 0)
    query_ids = lax.broadcasted_iota(jnp.int32, (block, block), 1)
    causal = key_ids <= query_ids

    def fold(x, op):
        return op(x.reshape(block // 8, 8, block), axis=0)

    for i in reversed(range(blocks)):
        rows = pl.ds(i * block, block)
        q_rows, g_rows = q[rows, :], g[rows, :]
        peak = jnp.full((8, block), -3.0e38, F32)
        for j in range(i + 1):
            cols = pl.ds(j * block, block)
            s = dot(k[cols, :], q_rows, ROWS_BY_ROWS)
            if j == i:
                s = jnp.where(causal, s, F32(-1e30))
            scores[cols, :] = s
            peak = jnp.maximum(peak, fold(s, jnp.max))
        peak = jnp.max(peak, axis=0, keepdims=True)
        total = jnp.zeros((8, block), F32)
        dots = jnp.zeros((8, block), F32)
        for j in range(i + 1):
            cols = pl.ds(j * block, block)
            e = jnp.exp2((scores[cols, :] - peak) * exponent)
            dp = dot(v[cols, :], g_rows, ROWS_BY_ROWS)
            scores[cols, :] = e
            slopes[cols, :] = dp
            total = total + fold(e, jnp.sum)
            dots = dots + fold(e * dp, jnp.sum)
        inverse = 1.0 / jnp.sum(total, axis=0, keepdims=True)
        row_dots = jnp.sum(dots, axis=0, keepdims=True) * inverse
        query_total = jnp.zeros((width, block), F32)
        for j in range(i + 1):
            cols = pl.ds(j * block, block)
            p = scores[cols, :] * inverse
            ds = (p * (slopes[cols, :] - row_dots)).astype(BF16)
            dv = dot(p.astype(BF16), g_rows, PLAIN)
            dk = dot(ds, q_rows, PLAIN)
            if i == blocks - 1:
                value_total[cols, :] = dv
                key_total[cols, :] = dk
            else:
                value_total[cols, :] += dv
                key_total[cols, :] += dk
            query_total = query_total + dot(k_turned[:, cols], ds, PLAIN)
        put(
            i,
            (query_total.T * scaling).astype(BF16),
            (key_total[rows, :] * scaling).astype(BF16),
            value_total[rows, :].astype(BF16),
        )


def kernel(
    sections, groups, heads, tokens, block,
    flag, far_src, own_src, grad_src, out,
    far, own, grad, sel, done, scores, slopes, key_total, value_total, k_turned,
    far_send, far_recv, own_send, own_recv, grad_send, grad_recv, out_send, out_recv,
):
    s = lax.axis_index("section")
    t = lax.axis_index("tp")
    mirror = sections - 1 - s
    length = groups * tokens
    mine = pl.ds(pl.multiple_of(t * tokens, tokens), tokens)

    barrier = pltpu.get_barrier_semaphore()

    def greet(i, _):
        peer = lax.bitwise_xor(t, i)
        pl.semaphore_signal(barrier, inc=1, device_id=(mirror, peer), device_id_type=MESH)

        @pl.when(i > 0)
        def _():
            pl.semaphore_signal(barrier, inc=1, device_id=(s, peer), device_id_type=MESH)

        return 0

    lax.fori_loop(0, groups, greet, 0)
    pl.semaphore_wait(barrier, 2 * groups - 1)

    def send_far(hd):
        def f(i, _):
            peer = lax.bitwise_xor(t, i)
            pltpu.make_async_remote_copy(
                src_ref=far_src.at[peer, hd], dst_ref=far.at[hd, :, mine, :],
                send_sem=far_send, recv_sem=far_recv.at[hd],
                device_id=(mirror, peer), device_id_type=MESH,
            ).start()
            return 0

        lax.fori_loop(0, groups, f, 0)

    def send_own(hd):
        pltpu.make_async_copy(own_src.at[t, hd], own.at[hd, :, mine, :], own_recv.at[hd]).start()
        pltpu.make_async_copy(grad_src.at[t, hd], grad.at[hd, mine, :], grad_recv.at[hd]).start()

        def f(i, _):
            peer = lax.bitwise_xor(t, i)
            pltpu.make_async_remote_copy(
                src_ref=own_src.at[peer, hd], dst_ref=own.at[hd, :, mine, :],
                send_sem=own_send, recv_sem=own_recv.at[hd],
                device_id=(s, peer), device_id_type=MESH,
            ).start()
            pltpu.make_async_remote_copy(
                src_ref=grad_src.at[peer, hd], dst_ref=grad.at[hd, mine, :],
                send_sem=grad_send, recv_sem=grad_recv.at[hd],
                device_id=(s, peer), device_id_type=MESH,
            ).start()
            return 0

        lax.fori_loop(1, groups, f, 0)

    for hd in range(heads):
        send_far(hd)
        send_own(hd)

    take_far = flag[0] != 0

    def one_head(hd, _):
        pltpu.make_async_copy(own.at[hd], own.at[hd], own_recv.at[hd]).wait()
        pltpu.make_async_copy(grad.at[hd], grad.at[hd], grad_recv.at[hd]).wait()
        pltpu.make_async_copy(far.at[hd], far.at[hd], far_recv.at[hd]).wait()

        def choose(n, _):
            rows = pl.ds(pl.multiple_of(n * block, block), block)
            sel[:, rows, :] = jnp.where(take_far, far[hd, :, rows, :], own[hd, :, rows, :])
            return 0

        lax.fori_loop(0, length // block, choose, 0)

        def put(i, dq, dk, dv):
            per = block // tokens
            for n in range(per):
                part = slice(n * tokens, (n + 1) * tokens)
                done[hd, i * per + n, 0] = dq[part]
                done[hd, i * per + n, 1] = dk[part]
                done[hd, i * per + n, 2] = dv[part]

        head_backward(
            sel.at[0], sel.at[1], sel.at[2], grad.at[hd], put,
            scores, slopes, key_total, value_total, k_turned, length, block,
        )
        pltpu.make_async_copy(done.at[hd, t], out.at[t, hd], out_recv).start()

        def f(i, _):
            peer = lax.bitwise_xor(t, i)
            pltpu.make_async_remote_copy(
                src_ref=done.at[hd, peer], dst_ref=out.at[t, hd],
                send_sem=out_send, recv_sem=out_recv,
                device_id=(s, peer), device_id_type=MESH,
            ).start()
            return 0

        lax.fori_loop(1, groups, f, 0)
        return 0

    lax.fori_loop(0, heads, one_head, 0)

    pltpu.make_async_copy(far_src, far_src, far_send).wait()
    rest = pl.ds(1, groups - 1)
    pltpu.make_async_copy(own_src.at[rest], own_src.at[rest], own_send).wait()
    pltpu.make_async_copy(grad_src.at[rest], grad_src.at[rest], grad_send).wait()
    pltpu.make_async_copy(out.at[rest], out.at[rest], out_send).wait()
    pltpu.make_async_copy(out, out, out_recv).wait()


def solution(mesh):
    sections, groups = mesh.shape["section"], mesh.shape["tp"]

    def local(saved_caches, keeper_code, result_slope):
        slots, tokens, triple, head_count, width = saved_caches.shape[1:]
        heads = head_count // groups
        length = groups * tokens
        block = 256
        s = lax.axis_index("section")
        home = keeper_code[s]
        away = keeper_code[sections - 1 - s]

        def slot(index):
            index = jnp.clip(index, 0, slots - 1)
            x = lax.dynamic_index_in_dim(saved_caches[0], index, 0, keepdims=False)
            x = x.reshape(tokens, triple, groups, heads, width)
            return jnp.transpose(x, (2, 3, 1, 0, 4))

        far_src = slot(away - slots)
        own_src = slot(home)
        grad_src = jnp.transpose(result_slope[0].reshape(tokens, groups, heads, width), (1, 2, 0, 3))
        flag = (home >= slots).astype(jnp.int32).reshape(1)
        anywhere = pl.BlockSpec(memory_space=pl.ANY)
        vmem = pltpu.VMEM
        sem = pltpu.SemaphoreType.DMA
        out = pl.pallas_call(
            functools.partial(kernel, sections, groups, heads, tokens, block),
            out_shape=jax.ShapeDtypeStruct((groups, heads, triple, tokens, width), BF16),
            in_specs=[pl.BlockSpec(memory_space=pltpu.SMEM), anywhere, anywhere, anywhere],
            out_specs=anywhere,
            scratch_shapes=[
                vmem((heads, triple, length, width), BF16),
                vmem((heads, triple, length, width), BF16),
                vmem((heads, length, width), BF16),
                vmem((triple, length, width), BF16),
                vmem((heads, groups, triple, tokens, width), BF16),
                vmem((length, block), F32),
                vmem((length, block), F32),
                vmem((length, width), F32),
                vmem((length, width), F32),
                vmem((width, length), BF16),
                sem, sem((heads,)), sem, sem((heads,)), sem, sem((heads,)), sem, sem,
            ],
            compiler_params=pltpu.CompilerParams(
                collective_id=0, has_side_effects=True, vmem_limit_bytes=48 * 2**20
            ),
        )(flag, far_src, own_src, grad_src)
        return jnp.transpose(out, (3, 2, 0, 1, 4)).reshape(1, tokens, triple, head_count, width)

    return jax.shard_map(
        local,
        mesh=mesh,
        in_specs=(P("section", None, "tp", None, None, None), P(), P("section", "tp", None, None)),
        out_specs=P("section", "tp", None, None, None),
        check_vma=False,
    )
```

time: 694 us -> 208 us (0.30)
  waiting for transfers between devices: 430 us -> 0 us
  Pallas kernels: 0 us -> 189 us
  matrix products: 85.8 us -> 0 us
  blocking collectives: 48.3 us -> 0 us
  local copies, waits for them, and re-layouts: 53.5 us -> 16.4 us
  other arithmetic: 35.5 us -> 0 us
  starting transfers between devices: 30.2 us -> 0 us
    ppermute x4 -> x0, waiting for transfers between devices: 393 us -> none  [from_partner(): return lax.ppermute(value, axis, pairs)]
    pallas_call x0 -> x1, Pallas kernels: none -> 189 us  [local(): pl.pallas_call(functools.partial(kernel, sections, groups, heads, tokens,...]
    dot_general x48 -> x0, matrix products: 85.8 us -> none  [the longest x8 25.1 us: step(): jnp.dot(score_grad.T, query_rows, preferred_element_type=jnp.float32)]
    all_to_all x1 -> x0, blocking collectives: 48.3 us -> none  [local(): lax.all_to_all(grads, 'tp', split_axis=0, concat_axis=2, tiled=True)]
    all_to_all x2 -> x0, waiting for transfers between devices: 37 us -> none  [the longest x1 37 us: local(): lax.all_to_all(chosen_groups, 'tp', split_axis=2, concat_axis=0, tiled=True)]
    while x145 -> x0, local copies, waits for them, and re-layouts: 27.1 us -> none
    div x8 -> x0, other arithmetic: 17 us -> none  [step(): probability = expo / jnp.sum(expo, axis=1, keepdims=True)]
    ppermute x4 -> x0, starting transfers between devices: 15.4 us -> none  [from_partner(): return lax.ppermute(value, axis, pairs)]
  transfers between devices with their start and end apart: 6 -> 0, of which waited for: 5 -> 0; matrix products, arithmetic and copies ran while one was open for 1% -> 0% of each run, Pallas kernels for 0% -> 0%
where the time goes in v1:
time: 208 us; the launch traced here: 207 us
  Pallas kernels  189 us (91%)
  local copies, waits for them, and re-layouts  16.4 us (8%)
    pallas_call x1, Pallas kernels, local(): pl.pallas_call(functools.partial(kernel, sections, groups, heads, tokens,...  189 us
    dynamic_slice x3, local copies, waits for them, and re-layouts, slot(): x = lax.dynamic_index_in_dim(saved_caches[0], index, 0, keepdims=False)  9.68 us

profile of v1, /device:TPU:1, one launch (start us, length us, event | category | flops | bytes accessed | tf_op | source)
XLA Modules:
  0.0 207.4 jit_solution(15242644740789910496)
XLA Ops:
  0.0 1.3 fusion
  3.3 1.6 copy.6
  4.9 3.9 %constant_dynamic-slice_fusion = (bf16[1,1,128,3,32,128]{5,4,3,2,1,0:T(8,128)(2,1)S(1)}, bf16[1,1,128,3,32,128]{5,4,3,2,1,0:T(8,128)(2,1)S(1)}) fusion(bf16[1,2,128,3,32,128]{5,4,3,2,1,0:T(8,128)(2,1)} %param.3, s32[]{:T(128)} %bitcast.3, s32[]{:T(128)} %bitcast), kind=kLoop, calls=%fused_computation | loop fusion | bytes 12582920 | tf_op jit(solution)/shard_map/jit(dynamic_index_in_dim)/dynamic_slice | solution.py:208
  8.8 2.9 %copy.5 = bf16[1,1,128,3,32,128]{5,2,3,4,1,0:T(8,128)(2,1)} copy(bf16[1,1,128,3,32,128]{5,4,3,2,1,0:T(8,128)(2,1)S(1)} %get-tuple-element.5) | data formatting | bytes 6291456 | tf_op jit(solution)/shard_map/jit(dynamic_index_in_dim)/dynamic_slice | solution.py:208
  11.7 2.9 %copy.4 = bf16[1,1,128,3,32,128]{5,2,3,4,1,0:T(8,128)(2,1)} copy(bf16[1,1,128,3,32,128]{5,4,3,2,1,0:T(8,128)(2,1)S(1)} %get-tuple-element.6) | data formatting | bytes 6291456 | tf_op jit(solution)/shard_map/jit(dynamic_index_in_dim)/dynamic_slice | solution.py:208
  14.6 189.1 %shard_map.37 = bf16[16,2,3,128,128]{4,3,2,1,0:T(8,128)(2,1)S(1)} custom-call(s32[1]{0:T(128)S(6)} %convert_element_type.4.flag, bf16[16,2,3,128,128]{4,3,2,1,0:T(8,128)(2,1)} %bitcast.17, bf16[16,2,3,128,128]{4,3,2,1,0:T(8,128)(2,1)} %bitcast.16, bf16[16,2,128,128]{3,2,1,0:T(8,128)(2,1)S(1)} %bitcast.15), custom_call_target="tpu_custom_call" | custom-call | tf_op jit(solution)/shard_map/pallas_call | solution.py:219
  203.7 3.7 %copy.7 = bf16[1,128,3,32,128]{4,3,2,1,0:T(8,128)(2,1)} copy(bf16[1,128,3,32,128]{4,1,2,3,0:T(8,128)(2,1)S(1)} %bitcast.14) | data formatting | bytes 6291456 | tf_op jit(solution)/shard_map/reshape | solution.py:241

commit v2 on v1

v2 whole, which is shorter than its diff:
```python
import functools

import jax
import jax.numpy as jnp
from jax import lax
from jax.experimental import pallas as pl
from jax.experimental.pallas import tpu as pltpu
from jax.sharding import PartitionSpec as P

MESH = pl.DeviceIdType.MESH
F32 = jnp.float32
BF16 = jnp.bfloat16
LOG2E = 1.4426950408889634
ROWS_BY_ROWS = (((1,), (1,)), ((), ()))
PLAIN = (((1,), (0,)), ((), ()))


def dot(a, b, dims):
    return lax.dot_general(a, b, dims, preferred_element_type=F32)


def fold(x, op):
    return op(x.reshape(x.shape[0] // 8, 8, x.shape[1]), axis=0)


def place(i, j):
    return i * (i + 1) // 2 + j


def softmax_and_value_grad(q, k, g, probs, value_total, put, length, block):
    exponent = q.shape[-1] ** (-0.5) * LOG2E
    blocks = length // block
    key_ids = lax.broadcasted_iota(jnp.int32, (block, block), 0)
    query_ids = lax.broadcasted_iota(jnp.int32, (block, block), 1)
    causal = key_ids <= query_ids
    for i in reversed(range(blocks)):
        rows = pl.ds(i * block, block)
        q_rows, g_rows = q[rows, :], g[rows, :]
        peak = jnp.full((8, block), -3.0e38, F32)
        for j in range(i + 1):
            s = dot(k[pl.ds(j * block, block), :], q_rows, ROWS_BY_ROWS)
            if j == i:
                s = jnp.where(causal, s, F32(-1e30))
            probs[place(i, j)] = s
            peak = jnp.maximum(peak, fold(s, jnp.max))
        peak = jnp.max(peak, axis=0, keepdims=True)
        total = jnp.zeros((8, block), F32)
        for j in range(i + 1):
            e = jnp.exp2((probs[place(i, j)] - peak) * exponent)
            probs[place(i, j)] = e
            total = total + fold(e, jnp.sum)
        inverse = 1.0 / jnp.sum(total, axis=0, keepdims=True)
        for j in range(i + 1):
            cols = pl.ds(j * block, block)
            p = probs[place(i, j)] * inverse
            probs[place(i, j)] = p
            dv = dot(p.astype(BF16), g_rows, PLAIN)
            if i == blocks - 1:
                value_total[cols, :] = dv
            else:
                value_total[cols, :] += dv
        put(i, value_total[rows, :].astype(BF16))


def query_and_key_grad(q, k, v, g, probs, slopes, key_total, k_turned, put, length, block, which):
    width = q.shape[-1]
    scaling = width ** (-0.5)
    blocks = length // block
    for i in which:
        rows = pl.ds(i * block, block)
        q_rows, g_rows = q[rows, :], g[rows, :]
        dots = jnp.zeros((8, block), F32)
        for j in range(i + 1):
            cols = pl.ds(j * block, block)
            dp = dot(v[cols, :], g_rows, ROWS_BY_ROWS)
            slopes[cols, :] = dp
            dots = dots + fold(probs[place(i, j)] * dp, jnp.sum)
        row_dots = jnp.sum(dots, axis=0, keepdims=True)
        query_total = jnp.zeros((width, block), F32)
        for j in range(i + 1):
            cols = pl.ds(j * block, block)
            ds = (probs[place(i, j)] * (slopes[cols, :] - row_dots)).astype(BF16)
            dk = dot(ds, q_rows, PLAIN)
            if i == blocks - 1:
                key_total[cols, :] = dk
            else:
                key_total[cols, :] += dk
            query_total = query_total + dot(k_turned[:, cols], ds, PLAIN)
        put(i, (query_total.T * scaling).astype(BF16), (key_total[rows, :] * scaling).astype(BF16))


def kernel(
    sections, groups, heads, tokens, block, slots,
    codes, store, slope, out,
    store_in0, store_in1, store_in2, slope_in, far_out, own_out, grad_out,
    far, own, grad, sel, done, probs, slopes, key_total, value_total, k_turned,
    load_sem, far_send, far_recv, own_send, own_recv, grad_send, grad_recv, out_send, out_recv,
):
    s = lax.axis_index("section")
    t = lax.axis_index("tp")
    mirror = sections - 1 - s
    length = groups * tokens
    triple = store.shape[2]
    mine = pl.ds(pl.multiple_of(t * tokens, tokens), tokens)
    step = 16
    store_in = (store_in0, store_in1, store_in2)

    def load(w):
        return pltpu.make_async_copy(store.at[:, :, w], store_in[w], load_sem.at[w])

    def load_slope():
        return pltpu.make_async_copy(slope, slope_in, load_sem.at[triple])

    for w in range(triple):
        load(w).start()
    load_slope().start()

    barrier = pltpu.get_barrier_semaphore()

    def greet(i, _):
        peer = lax.bitwise_xor(t, i)
        pl.semaphore_signal(barrier, inc=1, device_id=(mirror, peer), device_id_type=MESH)

        @pl.when(i > 0)
        def _():
            pl.semaphore_signal(barrier, inc=1, device_id=(s, peer), device_id_type=MESH)

        return 0

    lax.fori_loop(0, groups, greet, 0)
    home = codes[s]
    away = codes[mirror]
    own_slot = jnp.clip(home, 0, slots - 1)
    far_slot = jnp.clip(away - slots, 0, slots - 1)
    take_far = home >= slots

    def by_head(slot, w, to):
        def f(n, _):
            rows = pl.ds(pl.multiple_of(n * step, step), step)
            to[w, :, rows, :] = jnp.swapaxes(store_in[w][slot, rows], 0, 1)
            return 0

        lax.fori_loop(0, tokens // step, f, 0)

    def each_peer(first, f):
        def g(i, _):
            f(lax.bitwise_xor(t, i))
            return 0

        lax.fori_loop(first, groups, g, 0)

    def send_far(hd, w):
        def f(peer):
            pltpu.make_async_remote_copy(
                src_ref=far_out.at[w, peer * heads + hd], dst_ref=far.at[hd, w, mine, :],
                send_sem=far_send.at[hd, w], recv_sem=far_recv.at[hd, w],
                device_id=(mirror, peer), device_id_type=MESH,
            ).start()

        each_peer(0, f)

    def far_sent(hd, w):
        some = pl.ds(0, groups)
        pltpu.make_async_copy(far_out.at[w, some], far_out.at[w, some], far_send.at[hd, w]).wait()

    def far_here(hd, w):
        pltpu.make_async_copy(far.at[hd, w], far.at[hd, w], far_recv.at[hd, w]).wait()

    def send_own(hd):
        pltpu.make_async_copy(own_out.at[:, t * heads + hd], own.at[hd, :, mine, :], own_recv.at[hd]).start()
        pltpu.make_async_copy(grad_out.at[t * heads + hd], grad.at[hd, mine, :], grad_recv.at[hd]).start()

        def f(peer):
            pltpu.make_async_remote_copy(
                src_ref=own_out.at[:, peer * heads + hd], dst_ref=own.at[hd, :, mine, :],
                send_sem=own_send, recv_sem=own_recv.at[hd],
                device_id=(s, peer), device_id_type=MESH,
            ).start()
            pltpu.make_async_remote_copy(
                src_ref=grad_out.at[peer * heads + hd], dst_ref=grad.at[hd, mine, :],
                send_sem=grad_send, recv_sem=grad_recv.at[hd],
                device_id=(s, peer), device_id_type=MESH,
            ).start()

        each_peer(1, f)

    late = pl.ds(triple - 1, 1)
    early = pl.ds(0, triple - 1)
    last = triple - 1

    def slope_by_head(n, _):
        rows = pl.ds(pl.multiple_of(n * step, step), step)
        grad_out[:, rows, :] = jnp.swapaxes(slope_in[rows], 0, 1)
        return 0

    load(1).wait()
    by_head(far_slot, 1, far_out)
    pl.semaphore_wait(barrier, 2 * groups - 1)
    send_far(0, 1)
    load(0).wait()
    by_head(far_slot, 0, far_out)
    send_far(0, 0)
    load_slope().wait()
    lax.fori_loop(0, tokens // step, slope_by_head, 0)
    load(last).wait()
    for w in range(triple):
        by_head(own_slot, w, own_out)
    send_own(0)
    by_head(far_slot, last, far_out)
    send_far(0, last)
    for hd in range(1, heads):
        for w in (1, 0, last):
            send_far(hd, w)
        send_own(hd)

    def one_head(hd, _):
        pltpu.make_async_copy(own.at[hd], own.at[hd], own_recv.at[hd]).wait()
        pltpu.make_async_copy(grad.at[hd], grad.at[hd], grad_recv.at[hd]).wait()
        far_here(hd, 1)
        far_here(hd, 0)

        def choose(ws):
            def f(n, _):
                rows = pl.ds(pl.multiple_of(n * block, block), block)
                sel[ws, rows, :] = jnp.where(take_far, far[hd, ws, rows, :], own[hd, ws, rows, :])
                return 0

            lax.fori_loop(0, length // block, f, 0)

        per = block // tokens

        def put_value(i, dv):
            for n in range(per):
                done[hd, i * per + n, 2] = dv[n * tokens:(n + 1) * tokens]

        def put_query_key(i, dq, dk):
            for n in range(per):
                done[hd, i * per + n, 0] = dq[n * tokens:(n + 1) * tokens]
                done[hd, i * per + n, 1] = dk[n * tokens:(n + 1) * tokens]

        def give(peer, ws):
            @pl.when(peer == t)
            def _():
                pltpu.make_async_copy(done.at[hd, peer, ws], out.at[t, hd, ws], out_recv).start()

            @pl.when(peer != t)
            def _():
                pltpu.make_async_remote_copy(
                    src_ref=done.at[hd, peer, ws], dst_ref=out.at[t, hd, ws],
                    send_sem=out_send, recv_sem=out_recv,
                    device_id=(s, peer), device_id_type=MESH,
                ).start()

        choose(early)
        q, k, v, g = sel.at[0], sel.at[1], sel.at[2], grad.at[hd]
        k_turned[...] = k[...].T
        softmax_and_value_grad(q, k, g, probs, value_total, put_value, length, block)
        each_peer(0, lambda peer: give(peer, late))
        far_here(hd, last)
        choose(late)
        blocks = length // block
        half = groups // 2
        for part in (1, 0):
            which = reversed(range(part * blocks // 2, (part + 1) * blocks // 2))
            query_and_key_grad(
                q, k, v, g, probs, slopes, key_total, k_turned, put_query_key, length, block, which
            )

            def f(n, _):
                give(part * half + lax.rem(lax.bitwise_xor(t, n), half), early)
                return 0

            lax.fori_loop(0, half, f, 0)
        return 0

    lax.fori_loop(0, heads, one_head, 0)

    for hd in range(heads):
        for w in range(triple):
            far_sent(hd, w)
    sent = pl.ds(0, (groups - 1) * heads)
    pltpu.make_async_copy(own_out.at[:, sent], own_out.at[:, sent], own_send).wait()
    pltpu.make_async_copy(grad_out.at[sent], grad_out.at[sent], grad_send).wait()
    rest = pl.ds(1, groups - 1)
    pltpu.make_async_copy(out.at[rest], out.at[rest], out_send).wait()
    pltpu.make_async_copy(out, out, out_recv).wait()


def by_token(parts, whole, came, turned, load_sem, store_sem):
    groups, heads, triple, tokens, width = parts.shape
    step = 16
    loads = [pltpu.make_async_copy(parts.at[:, :, w], came.at[w], load_sem.at[w]) for w in range(triple)]
    stores = [pltpu.make_async_copy(turned.at[w], whole.at[:, w], store_sem.at[w]) for w in range(triple)]
    for load in loads:
        load.start()
    for w in range(triple):
        loads[w].wait()
        for n in range(tokens // step):
            rows = pl.ds(n * step, step)
            piece = came[w, :, :, rows, :].reshape(groups * heads, step, width)
            turned[w, rows] = jnp.swapaxes(piece, 0, 1)
        stores[w].start()
    for store in stores:
        store.wait()


def solution(mesh):
    sections, groups = mesh.shape["section"], mesh.shape["tp"]

    def local(saved_caches, keeper_code, result_slope):
        slots, tokens, triple, head_count, width = saved_caches.shape[1:]
        heads = head_count // groups
        length = groups * tokens
        block = 256
        blocks = length // block
        anywhere = pl.BlockSpec(memory_space=pl.ANY)
        vmem = pltpu.VMEM
        sem = pltpu.SemaphoreType.DMA
        out = pl.pallas_call(
            functools.partial(kernel, sections, groups, heads, tokens, block, slots),
            out_shape=jax.ShapeDtypeStruct((groups, heads, triple, tokens, width), BF16),
            in_specs=[pl.BlockSpec(memory_space=pltpu.SMEM), anywhere, anywhere],
            out_specs=anywhere,
            scratch_shapes=[
                *[vmem((slots, tokens, head_count, width), BF16)] * triple,
                vmem((tokens, head_count, width), BF16),
                vmem((triple, head_count, tokens, width), BF16),
                vmem((triple, head_count, tokens, width), BF16),
                vmem((head_count, tokens, width), BF16),
                vmem((heads, triple, length, width), BF16),
                vmem((heads, triple, length, width), BF16),
                vmem((heads, length, width), BF16),
                vmem((triple, length, width), BF16),
                vmem((heads, groups, triple, tokens, width), BF16),
                vmem((place(blocks, 0), block, block), F32),
                vmem((length, block), F32),
                vmem((length, width), F32),
                vmem((length, width), F32),
                vmem((width, length), BF16),
                sem((triple + 1,)),
                sem((heads, triple)), sem((heads, triple)), sem, sem((heads,)), sem, sem((heads,)), sem, sem,
            ],
            compiler_params=pltpu.CompilerParams(
                collective_id=0, has_side_effects=True, vmem_limit_bytes=56 * 2**20
            ),
        )(keeper_code, saved_caches[0], result_slope[0])
        whole = pl.pallas_call(
            by_token,
            out_shape=jax.ShapeDtypeStruct((tokens, triple, head_count, width), BF16),
            in_specs=[anywhere],
            out_specs=anywhere,
            scratch_shapes=[
                vmem((triple, groups, heads, tokens, width), BF16),
                vmem((triple, tokens, head_count, width), BF16),
                sem((triple,)), sem((triple,)),
            ],
            compiler_params=pltpu.CompilerParams(vmem_limit_bytes=56 * 2**20),
        )(out)
        return whole[None]

    return jax.shard_map(
        local,
        mesh=mesh,
        in_specs=(P("section", None, "tp", None, None, None), P(), P("section", "tp", None, None)),
        out_specs=P("section", "tp", None, None, None),
        check_vma=False,
    )
```

time: 208 us -> 184 us (0.88)
  local copies, waits for them, and re-layouts: 16.4 us -> 0 us
  Pallas kernels: 189 us -> 183 us
    dynamic_slice x4 -> x0, local copies, waits for them, and re-layouts: 11 us -> none  [the longest x3 9.68 us: slot(): x = lax.dynamic_index_in_dim(saved_caches[0], index, 0, keepdims=False)]
    pallas_call x1, Pallas kernels: 189 us -> 180 us  [local(): pl.pallas_call(functools.partial(kernel, sections, groups, heads, tokens,...]
    reshape x1 -> x0, local copies, waits for them, and re-layouts: 3.69 us -> none  [local(): jnp.transpose(out, (3, 2, 0, 1, 4))]
    pallas_call x0 -> x1, Pallas kernels: none -> 3.27 us  [local(): pl.pallas_call(by_token, out_shape=jax.ShapeDtypeStruct((tokens, triple,...]
where the time goes in v2:
time: 184 us; the launch traced here: 183 us
  Pallas kernels  183 us (99%)
    pallas_call x1, Pallas kernels, local(): pl.pallas_call(functools.partial(kernel, sections, groups, heads, tokens,...  180 us

profile of v2, /device:TPU:1, one launch (start us, length us, event | category | flops | bytes accessed | tf_op | source)
XLA Modules:
  0.0 183.4 jit_solution(16936706955182605186)
XLA Ops:
  0.0 180.2 %shard_map.37.parts = bf16[16,2,3,128,128]{4,3,2,1,0:T(8,128)(2,1)} custom-call(s32[16]{0:T(128)} %codes.1, bf16[2,128,3,32,128]{4,3,2,1,0:T(8,128)(2,1)} %bitcast.3, bf16[128,32,128]{2,1,0:T(8,128)(2,1)} %bitcast.4), custom_call_target="tpu_custom_call" | custom-call | tf_op jit(solution)/shard_map/pallas_call | solution.py:319
  180.2 3.3 %shard_map.38 = bf16[128,3,32,128]{3,2,1,0:T(8,128)(2,1)} custom-call(bf16[16,2,3,128,128]{4,3,2,1,0:T(8,128)(2,1)} %shard_map.37.parts), custom_call_target="tpu_custom_call" | custom-call | tf_op jit(solution)/shard_map/pallas_call | solution.py:347

commit v3 on v2

--- a/solution.py
+++ b/solution.py
@@ -21,6 +21,10 @@
 
 def fold(x, op):
     return op(x.reshape(x.shape[0] // 8, 8, x.shape[1]), axis=0)
+
+
+def chips_first(n):
+    return n % 4 * 2 + n // 4 % 2 + n // 8 * 8
 
 
 def place(i, j):
@@ -143,13 +147,13 @@
         lax.fori_loop(0, tokens // step, f, 0)
 
     def each_peer(first, f):
-        def g(i, _):
-            f(lax.bitwise_xor(t, i))
+        def g(n, _):
+            f(lax.bitwise_xor(t, chips_first(n)))
             return 0
 
         lax.fori_loop(first, groups, g, 0)
 
-    def send_far(hd, w):
+    def send_far(hd, w, classes=False):
         def f(peer):
             pltpu.make_async_remote_copy(
                 src_ref=far_out.at[w, peer * heads + hd], dst_ref=far.at[hd, w, mine, :],
@@ -157,7 +161,15 @@
                 device_id=(mirror, peer), device_id_type=MESH,
             ).start()
 
-        each_peer(0, f)
+        if classes:
+            def g(n, _):
+                order = n // 4
+                f(order % 2 * 8 + lax.bitwise_xor(t // 2 % 4, n % 4) * 2 + order // 2)
+                return 0
+
+            lax.fori_loop(0, groups, g, 0)
+        else:
+            each_peer(0, f)
 
     def far_sent(hd, w):
         some = pl.ds(0, groups)
@@ -209,9 +221,11 @@
     by_head(far_slot, last, far_out)
     send_far(0, last)
     for hd in range(1, heads):
-        for w in (1, 0, last):
-            send_far(hd, w)
         send_own(hd)
+    far_sent(0, 1)
+    send_far(1, 1)
+    far_sent(0, 0)
+    send_far(1, 0)
 
     def one_head(hd, _):
         pltpu.make_async_copy(own.at[hd], own.at[hd], own_recv.at[hd]).wait()
@@ -256,6 +270,12 @@
         k_turned[...] = k[...].T
         softmax_and_value_grad(q, k, g, probs, value_total, put_value, length, block)
         each_peer(0, lambda peer: give(peer, late))
+
+        @pl.when(hd + 1 < heads)
+        def _():
+            far_sent(hd, last)
+            send_far(hd + 1, last, classes=True)
+
         far_here(hd, last)
         choose(late)
         blocks = length // block
@@ -267,7 +287,7 @@
             )
 
             def f(n, _):
-                give(part * half + lax.rem(lax.bitwise_xor(t, n), half), early)
+                give(part * half + lax.rem(lax.bitwise_xor(t, chips_first(n)), half), early)
                 return 0
 
             lax.fori_loop(0, half, f, 0)
@@ -275,9 +295,8 @@
 
     lax.fori_loop(0, heads, one_head, 0)
 
-    for hd in range(heads):
-        for w in range(triple):
-            far_sent(hd, w)
+    for w in range(triple):
+        far_sent(heads - 1, w)
     sent = pl.ds(0, (groups - 1) * heads)
     pltpu.make_async_copy(own_out.at[:, sent], own_out.at[:, sent], own_send).wait()
     pltpu.make_async_copy(grad_out.at[sent], grad_out.at[sent], grad_send).wait()

time: 184 us -> 178 us (0.967)
  Pallas kernels: 183 us -> 178 us
    pallas_call x1, Pallas kernels: 180 us -> 175 us  [local(): pl.pallas_call(functools.partial(kernel, sections, groups, heads, tokens,...]
where the time goes in v3:
time: 178 us
  Pallas kernels  178 us (100%)
    pallas_call x1, Pallas kernels, local(): pl.pallas_call(functools.partial(kernel, sections, groups, heads, tokens,...  175 us

profile of v3, /device:TPU:1, one launch (start us, length us, event | category | flops | bytes accessed | tf_op | source)
XLA Modules:
  0.0 178.3 jit_solution(633682740068660721)
XLA Ops:
  0.0 175.1 %shard_map.37.parts = bf16[16,2,3,128,128]{4,3,2,1,0:T(8,128)(2,1)} custom-call(s32[16]{0:T(128)} %codes.1, bf16[2,128,3,32,128]{4,3,2,1,0:T(8,128)(2,1)} %bitcast.3, bf16[128,32,128]{2,1,0:T(8,128)(2,1)} %bitcast.4), custom_call_target="tpu_custom_call" | custom-call | tf_op jit(solution)/shard_map/pallas_call | solution.py:338
  175.1 3.3 %shard_map.38 = bf16[128,3,32,128]{3,2,1,0:T(8,128)(2,1)} custom-call(bf16[16,2,3,128,128]{4,3,2,1,0:T(8,128)(2,1)} %shard_map.37.parts), custom_call_target="tpu_custom_call" | custom-call | tf_op jit(solution)/shard_map/pallas_call | solution.py:366

commit v4 on v3

--- a/solution.py
+++ b/solution.py
@@ -66,24 +66,32 @@
         put(i, value_total[rows, :].astype(BF16))
 
 
-def query_and_key_grad(q, k, v, g, probs, slopes, key_total, k_turned, put, length, block, which):
+def query_and_key_grad(q, k, v, g, probs, slopes, key_total, k_turned, put, length, block):
     width = q.shape[-1]
     scaling = width ** (-0.5)
     blocks = length // block
-    for i in which:
-        rows = pl.ds(i * block, block)
-        q_rows, g_rows = q[rows, :], g[rows, :]
+
+    def ahead(i):
+        g_rows = g[pl.ds(i * block, block), :]
         dots = jnp.zeros((8, block), F32)
         for j in range(i + 1):
             cols = pl.ds(j * block, block)
             dp = dot(v[cols, :], g_rows, ROWS_BY_ROWS)
-            slopes[cols, :] = dp
+            slopes[i % 2, cols, :] = dp
             dots = dots + fold(probs[place(i, j)] * dp, jnp.sum)
-        row_dots = jnp.sum(dots, axis=0, keepdims=True)
+        return jnp.sum(dots, axis=0, keepdims=True)
+
+    next_dots = ahead(blocks - 1)
+    for i in reversed(range(blocks)):
+        rows = pl.ds(i * block, block)
+        q_rows = q[rows, :]
+        row_dots = next_dots
+        if i > 0:
+            next_dots = ahead(i - 1)
         query_total = jnp.zeros((width, block), F32)
         for j in range(i + 1):
             cols = pl.ds(j * block, block)
-            ds = (probs[place(i, j)] * (slopes[cols, :] - row_dots)).astype(BF16)
+            ds = (probs[place(i, j)] * (slopes[i % 2, cols, :] - row_dots)).astype(BF16)
             dk = dot(ds, q_rows, PLAIN)
             if i == blocks - 1:
                 key_total[cols, :] = dk
@@ -115,7 +123,7 @@
     def load_slope():
         return pltpu.make_async_copy(slope, slope_in, load_sem.at[triple])
 
-    for w in range(triple):
+    for w in (1, 0, 2):
         load(w).start()
     load_slope().start()
 
@@ -207,17 +215,17 @@
 
     load(1).wait()
     by_head(far_slot, 1, far_out)
+    load(0).wait()
+    by_head(far_slot, 0, far_out)
+    load(last).wait()
+    load_slope().wait()
+    for w in range(triple):
+        by_head(own_slot, w, own_out)
+    lax.fori_loop(0, tokens // step, slope_by_head, 0)
     pl.semaphore_wait(barrier, 2 * groups - 1)
     send_far(0, 1)
-    load(0).wait()
-    by_head(far_slot, 0, far_out)
+    send_own(0)
     send_far(0, 0)
-    load_slope().wait()
-    lax.fori_loop(0, tokens // step, slope_by_head, 0)
-    load(last).wait()
-    for w in range(triple):
-        by_head(own_slot, w, own_out)
-    send_own(0)
     by_head(far_slot, last, far_out)
     send_far(0, last)
     for hd in range(1, heads):
@@ -247,11 +255,6 @@
             for n in range(per):
                 done[hd, i * per + n, 2] = dv[n * tokens:(n + 1) * tokens]
 
-        def put_query_key(i, dq, dk):
-            for n in range(per):
-                done[hd, i * per + n, 0] = dq[n * tokens:(n + 1) * tokens]
-                done[hd, i * per + n, 1] = dk[n * tokens:(n + 1) * tokens]
-
         def give(peer, ws):
             @pl.when(peer == t)
             def _():
@@ -278,19 +281,21 @@
 
         far_here(hd, last)
         choose(late)
-        blocks = length // block
         half = groups // 2
-        for part in (1, 0):
-            which = reversed(range(part * blocks // 2, (part + 1) * blocks // 2))
-            query_and_key_grad(
-                q, k, v, g, probs, slopes, key_total, k_turned, put_query_key, length, block, which
-            )
-
-            def f(n, _):
-                give(part * half + lax.rem(lax.bitwise_xor(t, chips_first(n)), half), early)
-                return 0
-
-            lax.fori_loop(0, half, f, 0)
+
+        def put_query_key(i, dq, dk):
+            for n in range(per):
+                done[hd, i * per + n, 0] = dq[n * tokens:(n + 1) * tokens]
+                done[hd, i * per + n, 1] = dk[n * tokens:(n + 1) * tokens]
+            if i * per % half == 0:
+
+                def f(n, _):
+                    give(i * per + lax.rem(lax.bitwise_xor(t, chips_first(n)), half), early)
+                    return 0
+
+                lax.fori_loop(0, half, f, 0)
+
+        query_and_key_grad(q, k, v, g, probs, slopes, key_total, k_turned, put_query_key, length, block)
         return 0
 
     lax.fori_loop(0, heads, one_head, 0)
@@ -308,17 +313,22 @@
 def by_token(parts, whole, came, turned, load_sem, store_sem):
     groups, heads, triple, tokens, width = parts.shape
     step = 16
-    loads = [pltpu.make_async_copy(parts.at[:, :, w], came.at[w], load_sem.at[w]) for w in range(triple)]
-    stores = [pltpu.make_async_copy(turned.at[w], whole.at[:, w], store_sem.at[w]) for w in range(triple)]
+    chunk = tokens // 4
+    chunks = [(c, w) for c in range(tokens // chunk) for w in range(triple)]
+    loads, stores = [], []
+    for at, (c, w) in enumerate(chunks):
+        rows = pl.ds(c * chunk, chunk)
+        loads.append(pltpu.make_async_copy(parts.at[:, :, w, rows], came.at[c, w], load_sem.at[at]))
+        stores.append(pltpu.make_async_copy(turned.at[c, w], whole.at[rows, w], store_sem.at[at]))
     for load in loads:
         load.start()
-    for w in range(triple):
-        loads[w].wait()
-        for n in range(tokens // step):
+    for at, (c, w) in enumerate(chunks):
+        loads[at].wait()
+        for n in range(chunk // step):
             rows = pl.ds(n * step, step)
-            piece = came[w, :, :, rows, :].reshape(groups * heads, step, width)
-            turned[w, rows] = jnp.swapaxes(piece, 0, 1)
-        stores[w].start()
+            piece = came[c, w, :, :, rows, :].reshape(groups * heads, step, width)
+            turned[c, w, rows] = jnp.swapaxes(piece, 0, 1)
+        stores[at].start()
     for store in stores:
         store.wait()
 
@@ -352,7 +362,7 @@
                 vmem((triple, length, width), BF16),
                 vmem((heads, groups, triple, tokens, width), BF16),
                 vmem((place(blocks, 0), block, block), F32),
-                vmem((length, block), F32),
+                vmem((2, length, block), F32),
                 vmem((length, width), F32),
                 vmem((length, width), F32),
                 vmem((width, length), BF16),
@@ -369,9 +379,9 @@
             in_specs=[anywhere],
             out_specs=anywhere,
             scratch_shapes=[
-                vmem((triple, groups, heads, tokens, width), BF16),
-                vmem((triple, tokens, head_count, width), BF16),
-                sem((triple,)), sem((triple,)),
+                vmem((4, triple, groups, heads, tokens // 4, width), BF16),
+                vmem((4, triple, tokens // 4, head_count, width), BF16),
+                sem((4 * triple,)), sem((4 * triple,)),
             ],
             compiler_params=pltpu.CompilerParams(vmem_limit_bytes=56 * 2**20),
         )(out)

time: 178 us -> 176 us (0.989)
  Pallas kernels: 178 us -> 175 us
    pallas_call x1, Pallas kernels: 175 us -> 172 us  [local(): pl.pallas_call(functools.partial(kernel, sections, groups, heads, tokens,...]
where the time goes in v4:
time: 176 us; the launch traced here: 175 us
  Pallas kernels  175 us (99%)
    pallas_call x1, Pallas kernels, local(): pl.pallas_call(functools.partial(kernel, sections, groups, heads, tokens,...  172 us

profile of v4, /device:TPU:1, one launch (start us, length us, event | category | flops | bytes accessed | tf_op | source)
XLA Modules:
  0.0 174.6 jit_solution(7760095525408956629)
XLA Ops:
  0.0 171.7 %shard_map.37.parts = bf16[16,2,3,128,128]{4,3,2,1,0:T(8,128)(2,1)} custom-call(s32[16]{0:T(128)} %codes.1, bf16[2,128,3,32,128]{4,3,2,1,0:T(8,128)(2,1)} %bitcast.3, bf16[128,32,128]{2,1,0:T(8,128)(2,1)} %bitcast.4), custom_call_target="tpu_custom_call" | custom-call | tf_op jit(solution)/shard_map/pallas_call | solution.py:348
  171.7 2.9 %shard_map.38 = bf16[128,3,32,128]{3,2,1,0:T(8,128)(2,1)} custom-call(bf16[16,2,3,128,128]{4,3,2,1,0:T(8,128)(2,1)} %shard_map.37.parts), custom_call_target="tpu_custom_call" | custom-call | tf_op jit(solution)/shard_map/pallas_call | solution.py:376

commit v5 on v4

--- a/solution.py
+++ b/solution.py
@@ -106,7 +106,7 @@
     codes, store, slope, out,
     store_in0, store_in1, store_in2, slope_in, far_out, own_out, grad_out,
     far, own, grad, sel, done, probs, slopes, key_total, value_total, k_turned,
-    load_sem, far_send, far_recv, own_send, own_recv, grad_send, grad_recv, out_send, out_recv,
+    ready, load_sem, far_send, far_recv, own_send, own_recv, grad_send, grad_recv, out_send, out_recv,
 ):
     s = lax.axis_index("section")
     t = lax.axis_index("tp")
@@ -129,17 +129,30 @@
 
     barrier = pltpu.get_barrier_semaphore()
 
+    first = lax.rem(s, 4) < 2
+    second = lax.rem(s, 4) >= 2
+
     def greet(i, _):
         peer = lax.bitwise_xor(t, i)
-        pl.semaphore_signal(barrier, inc=1, device_id=(mirror, peer), device_id_type=MESH)
 
         @pl.when(i > 0)
         def _():
             pl.semaphore_signal(barrier, inc=1, device_id=(s, peer), device_id_type=MESH)
 
+        @pl.when(first)
+        def _():
+            pl.semaphore_signal(barrier, inc=1, device_id=(mirror, peer), device_id_type=MESH)
+
         return 0
 
     lax.fori_loop(0, groups, greet, 0)
+
+    def answer(i, _):
+        pl.semaphore_signal(
+            ready, inc=1, device_id=(mirror, lax.bitwise_xor(t, i)), device_id_type=MESH
+        )
+        return 0
+
     home = codes[s]
     away = codes[mirror]
     own_slot = jnp.clip(home, 0, slots - 1)
@@ -215,21 +228,48 @@
 
     load(1).wait()
     by_head(far_slot, 1, far_out)
+
+    @pl.when(second)
+    def _():
+        pl.semaphore_wait(barrier, 2 * groups - 1)
+        lax.fori_loop(0, groups, answer, 0)
+        send_far(0, 1)
+
     load(0).wait()
-    by_head(far_slot, 0, far_out)
     load(last).wait()
     load_slope().wait()
     for w in range(triple):
         by_head(own_slot, w, own_out)
     lax.fori_loop(0, tokens // step, slope_by_head, 0)
-    pl.semaphore_wait(barrier, 2 * groups - 1)
-    send_far(0, 1)
+
+    @pl.when(first)
+    def _():
+        pl.semaphore_wait(barrier, groups - 1)
+
     send_own(0)
-    send_far(0, 0)
+    by_head(far_slot, 0, far_out)
+
+    @pl.when(second)
+    def _():
+        send_far(0, 0)
+
     by_head(far_slot, last, far_out)
+
+    @pl.when(first)
+    def _():
+        for hd in range(1, heads):
+            send_own(hd)
+        pl.semaphore_wait(ready, groups)
+        send_far(0, 1)
+        send_far(0, 0)
+
     send_far(0, last)
-    for hd in range(1, heads):
-        send_own(hd)
+
+    @pl.when(second)
+    def _():
+        for hd in range(1, heads):
+            send_own(hd)
+
     far_sent(0, 1)
     send_far(1, 1)
     far_sent(0, 0)
@@ -366,6 +406,7 @@
                 vmem((length, width), F32),
                 vmem((length, width), F32),
                 vmem((width, length), BF16),
+                pltpu.SemaphoreType.REGULAR,
                 sem((triple + 1,)),
                 sem((heads, triple)), sem((heads, triple)), sem, sem((heads,)), sem, sem((heads,)), sem, sem,
             ],

time: 176 us -> 171 us (0.972); the launches traced: 175 us -> 168 us
  Pallas kernels: 175 us -> 168 us
    pallas_call x1, Pallas kernels: 172 us -> 165 us  [local(): pl.pallas_call(functools.partial(kernel, sections, groups, heads, tokens,...]
where the time goes in v5:
time: 171 us; the launch traced here: 168 us
  Pallas kernels  168 us (98%)
    pallas_call x1, Pallas kernels, local(): pl.pallas_call(functools.partial(kernel, sections, groups, heads, tokens,...  165 us

profile of v5, /device:TPU:1, one launch (start us, length us, event | category | flops | bytes accessed | tf_op | source)
XLA Modules:
  0.0 167.7 jit_solution(18245868110477599156)
XLA Ops:
  0.0 164.8 %shard_map.37.parts = bf16[16,2,3,128,128]{4,3,2,1,0:T(8,128)(2,1)} custom-call(s32[16]{0:T(128)} %codes.1, bf16[2,128,3,32,128]{4,3,2,1,0:T(8,128)(2,1)} %bitcast.3, bf16[128,32,128]{2,1,0:T(8,128)(2,1)} %bitcast.4), custom_call_target="tpu_custom_call" | custom-call | tf_op jit(solution)/shard_map/pallas_call | solution.py:388
  164.8 2.9 %shard_map.38 = bf16[128,3,32,128]{3,2,1,0:T(8,128)(2,1)} custom-call(bf16[16,2,3,128,128]{4,3,2,1,0:T(8,128)(2,1)} %shard_map.37.parts), custom_call_target="tpu_custom_call" | custom-call | tf_op jit(solution)/shard_map/pallas_call | solution.py:417

commit v6 on v5

--- a/solution.py
+++ b/solution.py
@@ -139,13 +139,12 @@
         def _():
             pl.semaphore_signal(barrier, inc=1, device_id=(s, peer), device_id_type=MESH)
 
-        @pl.when(first)
-        def _():
-            pl.semaphore_signal(barrier, inc=1, device_id=(mirror, peer), device_id_type=MESH)
-
+        pl.semaphore_signal(barrier, inc=1, device_id=(mirror, peer), device_id_type=MESH)
         return 0
 
-    lax.fori_loop(0, groups, greet, 0)
+    @pl.when(first)
+    def _():
+        lax.fori_loop(0, groups, greet, 0)
 
     def answer(i, _):
         pl.semaphore_signal(
@@ -226,13 +225,16 @@
         grad_out[:, rows, :] = jnp.swapaxes(slope_in[rows], 0, 1)
         return 0
 
+    @pl.when(second)
+    def _():
+        pl.semaphore_wait(barrier, groups)
+        lax.fori_loop(0, groups, answer, 0)
+
     load(1).wait()
     by_head(far_slot, 1, far_out)
 
     @pl.when(second)
     def _():
-        pl.semaphore_wait(barrier, 2 * groups - 1)
-        lax.fori_loop(0, groups, answer, 0)
         send_far(0, 1)
 
     load(0).wait()
@@ -246,13 +248,14 @@
     def _():
         pl.semaphore_wait(barrier, groups - 1)
 
+    by_head(far_slot, 0, far_out)
+
+    @pl.when(second)
+    def _():
+        send_far(0, 0)
+        pl.semaphore_wait(ready, 1)
+
     send_own(0)
-    by_head(far_slot, 0, far_out)
-
-    @pl.when(second)
-    def _():
-        send_far(0, 0)
-
     by_head(far_slot, last, far_out)
 
     @pl.when(first)
@@ -260,6 +263,7 @@
         for hd in range(1, heads):
             send_own(hd)
         pl.semaphore_wait(ready, groups)
+        pl.semaphore_signal(ready, inc=1, device_id=(mirror, t), device_id_type=MESH)
         send_far(0, 1)
         send_far(0, 0)
 

time: 171 us -> 170 us (level); the launches traced: 168 us -> 170 us
  Pallas kernels: 168 us -> 170 us
    pallas_call x1, Pallas kernels: 165 us -> 167 us  [local(): pl.pallas_call(functools.partial(kernel, sections, groups, heads, tokens,...]
where the time goes in v6:
time: 170 us
  Pallas kernels  170 us (100%)
    pallas_call x1, Pallas kernels, local(): pl.pallas_call(functools.partial(kernel, sections, groups, heads, tokens,...  167 us

profile of v6, /device:TPU:1, one launch (start us, length us, event | category | flops | bytes accessed | tf_op | source)
XLA Modules:
  0.0 170.0 jit_solution(6070096468328185341)
XLA Ops:
  0.0 167.1 %shard_map.37.parts = bf16[16,2,3,128,128]{4,3,2,1,0:T(8,128)(2,1)} custom-call(s32[16]{0:T(128)} %codes.1, bf16[2,128,3,32,128]{4,3,2,1,0:T(8,128)(2,1)} %bitcast.3, bf16[128,32,128]{2,1,0:T(8,128)(2,1)} %bitcast.4), custom_call_target="tpu_custom_call" | custom-call | tf_op jit(solution)/shard_map/pallas_call | solution.py:392
  167.1 2.9 %shard_map.38 = bf16[128,3,32,128]{3,2,1,0:T(8,128)(2,1)} custom-call(bf16[16,2,3,128,128]{4,3,2,1,0:T(8,128)(2,1)} %shard_map.37.parts), custom_call_target="tpu_custom_call" | custom-call | tf_op jit(solution)/shard_map/pallas_call | solution.py:421
